TPU v7x, 32 devices: a whole 2x2x4 slice. The times are simulated.
32 devices in a mesh: row: 16 (over z, x, core), col: 2 (over y).
Axes of the slice: x: 2, y: 2, z: 4, core: 2. Of those that a mesh axis runs over, the one named last changes fastest.
Arguments:
- vectors: bfloat16 [8, 32768], P(None, ('row', 'col')), may hold values from -6 to 6
- energies: float32 [32768], P(('row', 'col')), may hold values from 0.5 to 6
- tiles: bfloat16 [32768, 4096], P(('row', 'col')), may hold values from -0.25 to 0.25
- tile_rows: int32 [32768], P(('row', 'col')), may hold values from 0 to 31, as said below
- tile_cols: int32 [32768], P(('row', 'col')), may hold values from 0 to 255
- tile_count: int32 [32], P(('row', 'col')), may hold values from 128 to 1024, as said below
Outputs:
- product: bfloat16 [8, 32768], P(None, ('row', 'col'))
- residual: float32 [8, 32768], P(None, ('row', 'col'))
Inputs may be any that keep to these rules, and one draw needn't show every extreme that they name: `tile_count`: every count is at least 128, and some device uses all 1024 slots in every draw; a few devices are full while most use far fewer. `tile_rows`: slots may name the same row and column block more than once; such tiles add.
All inputs are finite; a program needn't handle non-finite values.
Results may differ from a plain program's by a relative error of at most 0.008.
Values may be sent and summed in bfloat16 or wider, within the bound.
No kernel may reach another device: no remote copies, remote signals or barrier semaphores. Data moves between devices by JAX's collectives and lax.ppermute only.
A program may use at most 64 MiB of HBM per device.

v0:
```python
import functools
import math

import jax
import jax.numpy as jnp
from jax import lax
from jax.experimental import pallas as pl
from jax.experimental.pallas import tpu as pltpu
from jax.sharding import Mesh, PartitionSpec as P

LANES = 128
SUB = 8
CHUNK = 128
STEP = 256
SUMS = 4

NT = (((1,), (1,)), ((), ()))


def tile_kernel(
    n_core, n_col, side, count_s, rows_h, cols_h, ener_h, tiles, *refs,
):
    gath, refs = refs[:n_core], refs[n_core:]
    (own_ref, send_ref, rest_ref, rows_s, cols_s, ener,
     buf, table, picked, select, part, sems, small, *acc) = refs
    n_far, kvec, own = gath[0].shape
    slots = tiles.shape[0]
    blk_own = own // side
    per = LANES // side
    n_chunk = tiles.shape[1] // LANES
    my_far, my_core, my_col = (lax.axis_index(name) for name in ("far", "core", "col"))

    copies = [
        pltpu.make_async_copy(src, dst, small.at[i])
        for i, (src, dst) in enumerate(
            ((cols_h, cols_s), (rows_h, rows_s), (ener_h, ener))
        )
    ]
    for copy in copies:
        copy.start()

    def tile_copy(ch):
        span = pl.ds(pl.multiple_of(ch * CHUNK, CHUNK), CHUNK)
        return pltpu.make_async_copy(tiles.at[span], buf.at[span], sems.at[ch])

    count = count_s[0]
    used = (count + CHUNK - 1) // CHUNK

    def ask(ch):
        @pl.when(ch < used)
        def _():
            tile_copy(ch).start()

    ahead = STEP // CHUNK
    for ch in range(ahead):
        ask(ch)

    lane = lax.broadcasted_iota(jnp.int32, (kvec, LANES), 1)
    low = lane < side
    zero = jnp.zeros((kvec, LANES), jnp.float32)

    for s in range(n_core):
        core = lax.rem(my_core + (n_core - s), n_core)
        for f in range(n_far):
            for p in range(own // LANES):
                x = gath[s][f, :, p * LANES:(p + 1) * LANES].astype(jnp.float32)
                y = pltpu.roll(x, side, 1)
                at = (f * n_core + core) * blk_own + p * per
                table[at] = jnp.where(low, x, y)
                table[at + 1] = jnp.where(low, y, x)
    n_blocks = n_far * n_core * blk_own
    table[n_blocks] = zero

    n_seg = acc[0].shape[0]
    width = n_chunk * SUB

    def clear(r, carry):
        for a in acc:
            a[r] = jnp.zeros(a.shape[1:], jnp.float32)
        return carry

    lax.fori_loop(0, n_seg, clear, 0)

    k_id = lax.broadcasted_iota(jnp.int32, (width, LANES), 0)
    n_id = lax.broadcasted_iota(jnp.int32, (width, LANES), 1)
    base_id = n_id - per * (k_id // SUB)
    for par in range(per):
        for jp in range(per):
            at = (par * per + jp) * width
            hit = (base_id == side * par + jp).astype(jnp.float32)
            select[at:at + width, :] = hit.astype(jnp.bfloat16)

    rows_of = per * kvec

    def product(base, half, x, check):
        xh = x[half * SUB:(half + 1) * SUB]
        w = jnp.concatenate(
            [xh[:, c * LANES:(c + 1) * LANES] for c in range(n_chunk)], axis=0
        ).astype(jnp.bfloat16)
        entries = []
        for t in range(SUB):
            slot = base + half * SUB + t
            at = cols_s[slot]
            entry = table[jnp.where(slot < count, at, n_blocks) if check else at]
            entries.append(jnp.where(low, entry, zero))
            entries.append(jnp.where(low, zero, entry))
        left = jnp.concatenate(entries, axis=0).astype(jnp.bfloat16)
        return lax.dot_general(left, w, NT, preferred_element_type=jnp.float32)

    lane_w = lax.broadcasted_iota(jnp.int32, (rows_of, width), 1) % SUB

    def accumulate(at, out):
        for t in range(SUB):
            r = rows_s[at + t]
            mine = jnp.where(lane_w == t, out[t * rows_of:(t + 1) * rows_of], 0.0)
            acc[t % len(acc)][r] += mine

    def step(first, slots_in, check):
        for i in range(slots_in // CHUNK):
            tile_copy(first // CHUNK + i).wait()
        waiting = None
        for q in range(slots_in // (2 * SUB)):
            base = pl.multiple_of(first + q * 2 * SUB, 2 * SUB)
            x = buf[pl.ds(base, 2 * SUB), :].astype(jnp.float32)
            for half in range(2):
                out = product(base, half, x, check)
                if waiting is not None:
                    accumulate(*waiting)
                waiting = (base + half * SUB, out)
        accumulate(*waiting)

    def full_step(i, carry):
        for ch in range(ahead):
            ask((i + 2) * ahead + ch)
        step(i * STEP, STEP, False)
        return carry

    def last_step(ch, carry):
        step(ch * CHUNK, CHUNK, True)
        return carry

    for ch in range(ahead, 2 * ahead):
        ask(ch)
    for copy in copies[:2]:
        copy.wait()
    full = count // STEP
    lax.fori_loop(0, full, full_step, 0)
    lax.fori_loop(full * (STEP // CHUNK), used, last_step, 0)

    pairs = n_seg // per

    def pick(m, carry):
        pieces = []
        for par in range(per):
            total = acc[0][m * per + par]
            for other in acc[1:]:
                total = total + other[m * per + par]
            for jp in range(per):
                pieces.append(total[jp * kvec:(jp + 1) * kvec])
        a = jnp.concatenate(pieces, axis=1)
        hi = a.astype(jnp.bfloat16).astype(jnp.float32)
        both = jnp.concatenate([hi, a - hi], axis=0).astype(jnp.bfloat16)
        picked[pl.ds(pl.multiple_of(m * 2 * kvec, 2 * kvec), 2 * kvec), :] = both
        return carry

    lax.fori_loop(0, pairs, pick, 0)

    spread = jnp.dot(picked[...], select[...], preferred_element_type=jnp.float32)
    for m in range(pairs):
        at = m * 2 * kvec
        row = spread[at:at + kvec] + spread[at + kvec:at + 2 * kvec]
        c, lane0 = divmod(m * LANES, own)
        part[c, :, lane0:lane0 + LANES] = row

    copies[2].wait()
    own_ref[...] = part[my_col] + ener[...] * gath[0][my_far].astype(jnp.float32)
    for s in range(1, n_col):
        share = part[lax.rem(my_col + s, n_col)]
        send_ref[s - 1] = share.astype(jnp.bfloat16)
        rest_ref[s - 1] = share


def tile_work(rows, cols, count, gath, n_col, ener, tiles):
    n_core = len(gath)
    n_far, kvec, own = gath[0].shape
    slots, area = tiles.shape
    side = math.isqrt(area)
    per = LANES // side
    blk_own = own // side
    n_seg = n_col * blk_own
    width = area // LANES * SUB
    vmem = pl.BlockSpec(memory_space=pltpu.VMEM)
    far_away = pl.BlockSpec(memory_space=pltpu.HBM)
    return pl.pallas_call(
        functools.partial(tile_kernel, n_core, n_col, side),
        out_shape=(
            jax.ShapeDtypeStruct((kvec, own), jnp.float32),
            jax.ShapeDtypeStruct((n_col - 1, kvec, own), jnp.bfloat16),
            jax.ShapeDtypeStruct((n_col - 1, kvec, own), jnp.float32),
        ),
        in_specs=[pl.BlockSpec(memory_space=pltpu.SMEM)] + [far_away] * 4 + [vmem] * n_core,
        out_specs=(vmem, vmem, vmem),
        scratch_shapes=[
            pltpu.SMEM((slots,), jnp.int32),
            pltpu.SMEM((slots,), jnp.int32),
            pltpu.VMEM((1, own), jnp.float32),
            pltpu.VMEM((slots, area), jnp.bfloat16),
            pltpu.VMEM((n_far * n_core * blk_own + 1, kvec, LANES), jnp.float32),
            pltpu.VMEM((n_seg // per * 2 * kvec, per * per * width), jnp.bfloat16),
            pltpu.VMEM((per * per * width, LANES), jnp.bfloat16),
            pltpu.VMEM((n_col, kvec, own), jnp.float32),
            pltpu.SemaphoreType.DMA((slots // CHUNK,)),
            pltpu.SemaphoreType.DMA((3,)),
        ] + [pltpu.VMEM((n_seg, per * kvec, width), jnp.float32)] * SUMS,
        compiler_params=pltpu.CompilerParams(vmem_limit_bytes=48 * 2**20),
        cost_estimate=pl.CostEstimate(
            flops=2 * slots * area * kvec, bytes_accessed=2 * slots * area, transcendentals=0
        ),
        name="tile_work",
    )(count, *[pltpu.with_memory_space_constraint(x, pltpu.HBM) for x in (rows, cols, ener, tiles)],
      *gath)


def terms_kernel(own, rest, vec, *refs):
    others, (terms_ref, wide) = refs[:-2], refs[-2:]
    n_col = len(others) + 1
    kvec = vec.shape[0]

    def outer(share, seg):
        return lax.dot_general(
            share, seg[...].astype(jnp.float32), NT,
            precision=lax.Precision.HIGHEST, preferred_element_type=jnp.float32,
        )

    terms = outer(own[...], vec)
    for s in range(1, n_col):
        terms = terms + outer(rest[s - 1], others[n_col - s - 1])
    wide[...] = jnp.zeros(wide.shape, jnp.float32)
    wide[:, :kvec] = terms
    spaced = pltpu.roll(wide[...], 0, 1, stride=kvec, stride_axis=0)
    terms_ref[...] = jnp.sum(spaced, axis=0, keepdims=True)


def gram_terms(own, rest, vectors, others):
    vmem = pl.BlockSpec(memory_space=pltpu.VMEM)
    return pl.pallas_call(
        terms_kernel,
        out_shape=jax.ShapeDtypeStruct((1, LANES), jnp.float32),
        in_specs=[vmem] * (3 + len(others)),
        out_specs=vmem,
        scratch_shapes=[pltpu.VMEM((vectors.shape[0], LANES), jnp.float32)],
        compiler_params=pltpu.CompilerParams(vmem_limit_bytes=4 * 2**20),
        name="gram_terms",
    )(own, rest, vectors, *others)


def finish_kernel(scale, base, gram_parts, vec, *refs):
    got, (product, residual) = refs[:-2], refs[-2:]
    whole = base[...]
    for piece in got:
        whole = whole + piece[...].astype(jnp.float32)
    product[...] = whole.astype(jnp.bfloat16)
    flat = gram_parts[0]
    for i in range(1, gram_parts.shape[0]):
        flat = flat + gram_parts[i]
    kvec = vec.shape[0]
    lane = lax.broadcasted_iota(jnp.int32, (kvec, LANES), 1)
    first = kvec * lax.broadcasted_iota(jnp.int32, (kvec, LANES), 0)
    wide = jnp.broadcast_to(flat * scale, (kvec, LANES))
    vec32 = vec[...].astype(jnp.float32)
    for a in range(kvec):
        column = jnp.sum(jnp.where(lane == first + a, wide, 0.0), axis=1, keepdims=True)
        whole = whole - column * vec32[a:a + 1, :]
    residual[...] = whole


def finish(scale, base, gram_parts, vectors, got):
    vmem = pl.BlockSpec(memory_space=pltpu.VMEM)
    return pl.pallas_call(
        functools.partial(finish_kernel, scale),
        out_shape=(
            jax.ShapeDtypeStruct(vectors.shape, jnp.bfloat16),
            jax.ShapeDtypeStruct(vectors.shape, jnp.float32),
        ),
        in_specs=[vmem] * (3 + len(got)),
        out_specs=(vmem, vmem),
        compiler_params=pltpu.CompilerParams(vmem_limit_bytes=4 * 2**20),
        name="finish",
    )(base, gram_parts, vectors, *got)


def from_all(x, axis):
    size = lax.axis_size(axis)
    got = [x]
    for s in range(1, size):
        got.append(lax.ppermute(x, axis, [(i, (i + s) % size) for i in range(size)]))
    return got


def per_device(vectors, energies, tiles, tile_rows, tile_cols, tile_count):
    kvec, own = vectors.shape
    n_col = lax.axis_size("col")
    copies = jnp.broadcast_to(vectors[None], (lax.axis_size("far"), kvec, own))
    gath = lax.all_to_all(copies, "far", 0, 0)
    gath = from_all(gath, "core")
    base, send, rest = tile_work(
        tile_rows, tile_cols, tile_count, gath, n_col, energies[None, :], tiles
    )
    got = [
        lax.ppermute(send[s - 1], "col", [(c, (c + s) % n_col) for c in range(n_col)])
        for s in range(1, n_col)
    ]
    others = from_all(vectors, "col")[1:]
    members = lax.axis_size(("far", "core", "col"))
    terms = gram_terms(base, rest, vectors, others)
    terms = jnp.broadcast_to(terms[None], (members,) + terms.shape)
    gram_parts = lax.all_to_all(terms, ("far", "core", "col"), 0, 0)
    return finish(1.0 / (members * own), base, gram_parts, vectors, got)


def solution(mesh):
    n_row, n_col = mesh.devices.shape
    n_core = 2 if n_row % 2 == 0 else 1
    split = ("far", "core", "col")
    chips = Mesh(mesh.devices.reshape(n_row // n_core, n_core, n_col), split)
    in_specs = (P(None, split), P(split), P(split, None), P(split), P(split), P(split))
    out_specs = (P(None, split), P(None, split))
    return jax.shard_map(
        per_device, mesh=chips, in_specs=in_specs, out_specs=out_specs, check_vma=False
    )
```

profile of v0, /device:TPU:0, one launch (start us, length us, event | category | flops | bytes accessed | tf_op | source)
XLA Modules:
  0.0 33.7 jit_solution(16568952750335914943)
XLA Ops:
  0.6 0.0 copy-start
  0.6 0.8 %broadcast_in_dim.18 = bf16[8,8,1024]{2,1,0:T(8,128)(2,1)S(1)} broadcast(bf16[8,1024]{1,0:T(8,128)(2,1)} %vec.3), dimensions={1,2} | broadcast | bytes 147456 | tf_op jit(solution)/shard_map/broadcast_in_dim | solution.py:303
  1.4 14.4 %all_to_all.10.refs_0_ = bf16[8,8,1024]{2,1,0:T(8,128)(2,1)S(1)} all-to-all(bf16[8,8,1024]{2,1,0:T(8,128)(2,1)S(1)} %broadcast_in_dim.18), channel_id=1, replica_groups=mesh['far'=8,'core'=2,'col'=2] {'far'}, dimensions={0} | all-to-all | bytes 262144 | tf_op jit(solution)/shard_map/all_to_all | solution.py:304
  15.8 0.0 collective-permute-start
  15.8 1.5 %collective-permute-start.1 = (bf16[8,1024]{1,0:T(8,128)(2,1)}, bf16[8,1024]{1,0:T(8,128)(2,1)S(1)}, u32[]{:S(2)}, u32[]{:S(2)}) collective-permute-start(bf16[8,1024]{1,0:T(8,128)(2,1)} %vec.3), channel_id=1, source_target_pairs={{0,1},{1,0},{2,3},{3,2},{4,5},{5,4},{6,7},{7,6},{8,9},{9,8},{10,11... | collective-permute-start | bytes 49160 | tf_op jit(solution)/shard_map/ppermute | solution.py:296
  18.0 0.0 collective-permute-done.refs_1_
  18.0 3.6 %tile_work.1 = (f32[8,1024]{1,0:T(8,128)S(1)}, bf16[1,8,1024]{2,1,0:T(8,128)(2,1)S(1)}, f32[1,8,1024]{2,1,0:T(8,128)S(1)}) custom-call(s32[1]{0:T(128)S(6)} %copy.8.count_s, s32[1024]{0:T(1024)} %rows_h.1, s32[1024]{0:T(1024)} %cols_h.1, f32[1,1024]{1,0:T(1,128)} %bitcast.5, bf16[1024,4096]{1,0:T(8,128)(2,1)} %tiles.1, ...), custom_call_target="tpu_custom_call" | custom-call | flops 67108864 | bytes 8388608 | tf_op jit(solution)/shard_map/tile_work/pallas_call | solution.py:194
  21.6 0.0 collective-permute-done.1.refs_0_
  21.6 0.0 copy-done
  21.6 0.3 gram_terms.1
  21.9 0.6 %broadcast_in_dim.20 = f32[32,1,128]{2,1,0:T(1,128)} broadcast(f32[128]{0:T(128)S(1)} %bitcast.3), dimensions={2} | broadcast | bytes 16896 | tf_op jit(solution)/shard_map/broadcast_in_dim | solution.py:316
  22.6 3.2 %all-to-all-start.1 = ((f32[32,1,128]{2,1,0:T(1,128)}), f32[32,1,128]{2,1,0:T(1,128)S(1)}, u32[]{:S(2)}, u32[]{:S(2)}) async-start(f32[32,1,128]{2,1,0:T(1,128)} %broadcast_in_dim.20), calls=%async_computation.1 | async-start | bytes 32768 | tf_op jit(solution)/shard_map/all_to_all | solution.py:317
  25.8 1.8 %collective-permute-start.2 = (bf16[8,1024]{1,0:T(8,128)(2,1)S(1)}, bf16[8,1024]{1,0:T(8,128)(2,1)S(1)}, u32[]{:S(2)}, u32[]{:S(2)}) collective-permute-start(bf16[8,1024]{1,0:T(8,128)(2,1)S(1)} %bitcast.4), channel_id=1, source_target_pairs={{0,1},{1,0},{2,3},{3,2},{4,5},{5,4},{6,7},{7,6},{8,9},{9,8},{10,11... | collective-permute-start | bytes 49160 | tf_op jit(solution)/shard_map/ppermute | solution.py:310
  27.7 2.0 %collective-permute-done.2.refs_0_ = bf16[8,1024]{1,0:T(8,128)(2,1)S(1)} collective-permute-done((bf16[8,1024]{1,0:T(8,128)(2,1)S(1)}, bf16[8,1024]{1,0:T(8,128)(2,1)S(1)}, u32[]{:S(2)}, u32[]{:S(2)}) %collective-permute-start.2) | collective-permute-done | bytes 16416 | tf_op jit(solution)/shard_map/ppermute | solution.py:310
  29.7 3.3 %all-to-all-done.1.gram_parts = f32[32,1,128]{2,1,0:T(1,128)S(1)} async-done(((f32[32,1,128]{2,1,0:T(1,128)}), f32[32,1,128]{2,1,0:T(1,128)S(1)}, u32[]{:S(2)}, u32[]{:S(2)}) %all-to-all-start.1) | async-done | bytes 16416 | tf_op jit(solution)/shard_map/all_to_all | solution.py:317
  33.0 0.8 %finish.1 = (bf16[8,1024]{1,0:T(8,128)(2,1)}, f32[8,1024]{1,0:T(8,128)}) custom-call(f32[8,1024]{1,0:T(8,128)S(1)} %get-tuple-element.5.own.base, f32[32,1,128]{2,1,0:T(1,128)S(1)} %all-to-all-done.1.gram_parts, bf16[8,1024]{1,0:T(8,128)(2,1)S(1)} %copy-done, bf16[8,1024]{1,0:T(8,128)(2,1)S(1)} %collective-permute-done.2.refs_0_), custom_call_target="tpu_custom_call" | custom-call | tf_op jit(solution)/shard_map/finish/pallas_call | solution.py:279
Async XLA Ops:
  0.6 21.0 %copy-start = (bf16[8,1024]{1,0:T(8,128)(2,1)S(1)}, bf16[8,1024]{1,0:T(8,128)(2,1)}, u32[]{:S(2)}) copy-start(bf16[8,1024]{1,0:T(8,128)(2,1)} %vec.3) | copy-start | bytes 49156
  15.8 2.2 %collective-permute-start = (bf16[8,8,1024]{2,1,0:T(8,128)(2,1)S(1)}, bf16[8,8,1024]{2,1,0:T(8,128)(2,1)S(1)}, u32[]{:S(2)}, u32[]{:S(2)}) collective-permute-start(bf16[8,8,1024]{2,1,0:T(8,128)(2,1)S(1)} %all_to_all.10.refs_0_), channel_id=1, source_target_pairs={{0,2},{2,0},{1,3},{3,1},{4,6},{6,4},{5,7},{7,5},{8,10},{10,8},{9,1... | collective-permute-start | bytes 393224 | tf_op jit(solution)/shard_map/ppermute | solution.py:296
  15.8 5.8 %collective-permute-start.1 = (bf16[8,1024]{1,0:T(8,128)(2,1)}, bf16[8,1024]{1,0:T(8,128)(2,1)S(1)}, u32[]{:S(2)}, u32[]{:S(2)}) collective-permute-start(bf16[8,1024]{1,0:T(8,128)(2,1)} %vec.3), channel_id=1, source_target_pairs={{0,1},{1,0},{2,3},{3,2},{4,5},{5,4},{6,7},{7,6},{8,9},{9,8},{10,11... | collective-permute-start | bytes 49160 | tf_op jit(solution)/shard_map/ppermute | solution.py:296
  22.6 10.4 %all-to-all-start.1 = ((f32[32,1,128]{2,1,0:T(1,128)}), f32[32,1,128]{2,1,0:T(1,128)S(1)}, u32[]{:S(2)}, u32[]{:S(2)}) async-start(f32[32,1,128]{2,1,0:T(1,128)} %broadcast_in_dim.20), calls=%async_computation.1 | async-start | bytes 32768 | tf_op jit(solution)/shard_map/all_to_all | solution.py:317
  25.8 3.8 %collective-permute-start.2 = (bf16[8,1024]{1,0:T(8,128)(2,1)S(1)}, bf16[8,1024]{1,0:T(8,128)(2,1)S(1)}, u32[]{:S(2)}, u32[]{:S(2)}) collective-permute-start(bf16[8,1024]{1,0:T(8,128)(2,1)S(1)} %bitcast.4), channel_id=1, source_target_pairs={{0,1},{1,0},{2,3},{3,2},{4,5},{5,4},{6,7},{7,6},{8,9},{9,8},{10,11... | collective-permute-start | bytes 49160 | tf_op jit(solution)/shard_map/ppermute | solution.py:310
where the time goes:
time: 34 us; the launch traced here: 33.7 us
  blocking collectives  14.4 us (42%)
  starting transfers between devices  6.6 us (19%)
  waiting for transfers between devices  5.29 us (16%)
  Pallas kernels  4.65 us (14%)
  local copies, waits for them, and re-layouts  1.43 us (4%)
  between operations  1.33 us (4%)
    all_to_all x1, blocking collectives, per_device(): gath = lax.all_to_all(copies, 'far', 0, 0)  14.4 us
    pallas_call x1, Pallas kernels, tile_work(): pl.pallas_call(functools.partial(tile_kernel, n_core, n_col, side), out_s...  3.58 us
    all_to_all x1, waiting for transfers between devices, per_device(): gram_parts = lax.all_to_all(terms, ('far', 'core', 'col'), 0, 0)  3.3 us
    all_to_all x1, starting transfers between devices, per_device(): gram_parts = lax.all_to_all(terms, ('far', 'core', 'col'), 0, 0)  3.25 us
    ppermute x1, waiting for transfers between devices, per_device(): lax.ppermute(send[s - 1], 'col', [(c, (c + s) % n_col) for c in range(n_c...  1.99 us
    ppermute x1, starting transfers between devices, per_device(): lax.ppermute(send[s - 1], 'col', [(c, (c + s) % n_col) for c in range(n_c...  1.83 us
    ppermute x2, starting transfers between devices, from_all(): lax.ppermute(x, axis, [(i, (i + s) % size) for i in range(size)])  1.52 us
    broadcast_in_dim x1, local copies, waits for them, and re-layouts, per_device(): copies = jnp.broadcast_to(vectors[None], (lax.axis_size('far'), kvec, own))  0.79 us
  transfers between devices with their start and end apart: 4, of which 2 were waited for; matrix products, arithmetic and copies ran while one was open for 0% of the time, Pallas kernels for 11%

commit v1 on v0

--- a/solution.py
+++ b/solution.py
@@ -105,7 +105,7 @@
             entries.append(jnp.where(low, entry, zero))
             entries.append(jnp.where(low, zero, entry))
         left = jnp.concatenate(entries, axis=0).astype(jnp.bfloat16)
-        return lax.dot_general(left, w, NT, preferred_element_type=jnp.float32)
+        return jnp.dot(left, w.T, preferred_element_type=jnp.float32)
 
     lane_w = lax.broadcasted_iota(jnp.int32, (rows_of, width), 1) % SUB
 

time: 34 us -> 34 us (level)
  starting transfers between devices: 6.6 us -> 7.25 us
  Pallas kernels: 4.65 us -> 4.01 us
    all_to_all x1, starting transfers between devices: 3.25 us -> 3.89 us  [per_device(): gram_parts = lax.all_to_all(terms, ('far', 'core', 'col'), 0, 0)]
    pallas_call x1, Pallas kernels: 3.58 us -> 2.94 us  [tile_work(): pl.pallas_call(functools.partial(tile_kernel, n_core, n_col, side), out_s...]
  transfers between devices with their start and end apart: 4 -> 4, of which waited for: 2 -> 2; matrix products, arithmetic and copies ran while one was open for 0% -> 0% of each run, Pallas kernels for 11% -> 9%
where the time goes in v1:
time: 34 us; the launch traced here: 33.7 us
  blocking collectives  14.4 us (42%)
  starting transfers between devices  7.25 us (21%)
  waiting for transfers between devices  5.29 us (16%)
  Pallas kernels  4.01 us (12%)
  local copies, waits for them, and re-layouts  1.43 us (4%)
  between operations  1.33 us (4%)
    all_to_all x1, blocking collectives, per_device(): gath = lax.all_to_all(copies, 'far', 0, 0)  14.4 us
    all_to_all x1, starting transfers between devices, per_device(): gram_parts = lax.all_to_all(terms, ('far', 'core', 'col'), 0, 0)  3.89 us
    all_to_all x1, waiting for transfers between devices, per_device(): gram_parts = lax.all_to_all(terms, ('far', 'core', 'col'), 0, 0)  3.3 us
    pallas_call x1, Pallas kernels, tile_work(): pl.pallas_call(functools.partial(tile_kernel, n_core, n_col, side), out_s...  2.94 us
    ppermute x1, waiting for transfers between devices, per_device(): lax.ppermute(send[s - 1], 'col', [(c, (c + s) % n_col) for c in range(n_c...  1.99 us
    ppermute x1, starting transfers between devices, per_device(): lax.ppermute(send[s - 1], 'col', [(c, (c + s) % n_col) for c in range(n_c...  1.83 us
    ppermute x2, starting transfers between devices, from_all(): lax.ppermute(x, axis, [(i, (i + s) % size) for i in range(size)])  1.52 us
    broadcast_in_dim x1, local copies, waits for them, and re-layouts, per_device(): copies = jnp.broadcast_to(vectors[None], (lax.axis_size('far'), kvec, own))  0.79 us
  transfers between devices with their start and end apart: 4, of which 2 were waited for; matrix products, arithmetic and copies ran while one was open for 0% of the time, Pallas kernels for 9%

profile of v1, /device:TPU:0, one launch (start us, length us, event | category | flops | bytes accessed | tf_op | source)
XLA Modules:
  0.0 33.7 jit_solution(16568952750335914943)
XLA Ops:
  0.6 0.0 copy-start
  0.6 0.8 %broadcast_in_dim.18 = bf16[8,8,1024]{2,1,0:T(8,128)(2,1)S(1)} broadcast(bf16[8,1024]{1,0:T(8,128)(2,1)} %vec.3), dimensions={1,2} | broadcast | bytes 147456 | tf_op jit(solution)/shard_map/broadcast_in_dim | solution.py:303
  1.4 14.4 %all_to_all.10.refs_0_ = bf16[8,8,1024]{2,1,0:T(8,128)(2,1)S(1)} all-to-all(bf16[8,8,1024]{2,1,0:T(8,128)(2,1)S(1)} %broadcast_in_dim.18), channel_id=1, replica_groups=mesh['far'=8,'core'=2,'col'=2] {'far'}, dimensions={0} | all-to-all | bytes 262144 | tf_op jit(solution)/shard_map/all_to_all | solution.py:304
  15.8 0.0 collective-permute-start
  15.8 1.5 %collective-permute-start.1 = (bf16[8,1024]{1,0:T(8,128)(2,1)}, bf16[8,1024]{1,0:T(8,128)(2,1)S(1)}, u32[]{:S(2)}, u32[]{:S(2)}) collective-permute-start(bf16[8,1024]{1,0:T(8,128)(2,1)} %vec.3), channel_id=1, source_target_pairs={{0,1},{1,0},{2,3},{3,2},{4,5},{5,4},{6,7},{7,6},{8,9},{9,8},{10,11... | collective-permute-start | bytes 49160 | tf_op jit(solution)/shard_map/ppermute | solution.py:296
  18.0 0.0 collective-permute-done.refs_1_
  18.0 2.9 %tile_work.1 = (f32[8,1024]{1,0:T(8,128)S(1)}, bf16[1,8,1024]{2,1,0:T(8,128)(2,1)S(1)}, f32[1,8,1024]{2,1,0:T(8,128)S(1)}) custom-call(s32[1]{0:T(128)S(6)} %copy.8.count_s, s32[1024]{0:T(1024)} %rows_h.1, s32[1024]{0:T(1024)} %cols_h.1, f32[1,1024]{1,0:T(1,128)} %bitcast.5, bf16[1024,4096]{1,0:T(8,128)(2,1)} %tiles.1, ...), custom_call_target="tpu_custom_call" | custom-call | flops 67108864 | bytes 8388608 | tf_op jit(solution)/shard_map/tile_work/pallas_call | solution.py:194
  21.0 0.0 collective-permute-done.1.refs_0_
  21.0 0.0 copy-done
  21.0 0.3 gram_terms.1
  21.3 0.6 %broadcast_in_dim.20 = f32[32,1,128]{2,1,0:T(1,128)} broadcast(f32[128]{0:T(128)S(1)} %bitcast.3), dimensions={2} | broadcast | bytes 16896 | tf_op jit(solution)/shard_map/broadcast_in_dim | solution.py:316
  21.9 3.9 %all-to-all-start.1 = ((f32[32,1,128]{2,1,0:T(1,128)}), f32[32,1,128]{2,1,0:T(1,128)S(1)}, u32[]{:S(2)}, u32[]{:S(2)}) async-start(f32[32,1,128]{2,1,0:T(1,128)} %broadcast_in_dim.20), calls=%async_computation.1 | async-start | bytes 32768 | tf_op jit(solution)/shard_map/all_to_all | solution.py:317
  25.8 1.8 %collective-permute-start.2 = (bf16[8,1024]{1,0:T(8,128)(2,1)S(1)}, bf16[8,1024]{1,0:T(8,128)(2,1)S(1)}, u32[]{:S(2)}, u32[]{:S(2)}) collective-permute-start(bf16[8,1024]{1,0:T(8,128)(2,1)S(1)} %bitcast.4), channel_id=1, source_target_pairs={{0,1},{1,0},{2,3},{3,2},{4,5},{5,4},{6,7},{7,6},{8,9},{9,8},{10,11... | collective-permute-start | bytes 49160 | tf_op jit(solution)/shard_map/ppermute | solution.py:310
  27.7 2.0 %collective-permute-done.2.refs_0_ = bf16[8,1024]{1,0:T(8,128)(2,1)S(1)} collective-permute-done((bf16[8,1024]{1,0:T(8,128)(2,1)S(1)}, bf16[8,1024]{1,0:T(8,128)(2,1)S(1)}, u32[]{:S(2)}, u32[]{:S(2)}) %collective-permute-start.2) | collective-permute-done | bytes 16416 | tf_op jit(solution)/shard_map/ppermute | solution.py:310
  29.7 3.3 %all-to-all-done.1.gram_parts = f32[32,1,128]{2,1,0:T(1,128)S(1)} async-done(((f32[32,1,128]{2,1,0:T(1,128)}), f32[32,1,128]{2,1,0:T(1,128)S(1)}, u32[]{:S(2)}, u32[]{:S(2)}) %all-to-all-start.1) | async-done | bytes 16416 | tf_op jit(solution)/shard_map/all_to_all | solution.py:317
  33.0 0.8 %finish.1 = (bf16[8,1024]{1,0:T(8,128)(2,1)}, f32[8,1024]{1,0:T(8,128)}) custom-call(f32[8,1024]{1,0:T(8,128)S(1)} %get-tuple-element.5.own.base, f32[32,1,128]{2,1,0:T(1,128)S(1)} %all-to-all-done.1.gram_parts, bf16[8,1024]{1,0:T(8,128)(2,1)S(1)} %copy-done, bf16[8,1024]{1,0:T(8,128)(2,1)S(1)} %collective-permute-done.2.refs_0_), custom_call_target="tpu_custom_call" | custom-call | tf_op jit(solution)/shard_map/finish/pallas_call | solution.py:279
Async XLA Ops:
  0.6 20.3 %copy-start = (bf16[8,1024]{1,0:T(8,128)(2,1)S(1)}, bf16[8,1024]{1,0:T(8,128)(2,1)}, u32[]{:S(2)}) copy-start(bf16[8,1024]{1,0:T(8,128)(2,1)} %vec.3) | copy-start | bytes 49156
  15.8 2.2 %collective-permute-start = (bf16[8,8,1024]{2,1,0:T(8,128)(2,1)S(1)}, bf16[8,8,1024]{2,1,0:T(8,128)(2,1)S(1)}, u32[]{:S(2)}, u32[]{:S(2)}) collective-permute-start(bf16[8,8,1024]{2,1,0:T(8,128)(2,1)S(1)} %all_to_all.10.refs_0_), channel_id=1, source_target_pairs={{0,2},{2,0},{1,3},{3,1},{4,6},{6,4},{5,7},{7,5},{8,10},{10,8},{9,1... | collective-permute-start | bytes 393224 | tf_op jit(solution)/shard_map/ppermute | solution.py:296
  15.8 5.1 %collective-permute-start.1 = (bf16[8,1024]{1,0:T(8,128)(2,1)}, bf16[8,1024]{1,0:T(8,128)(2,1)S(1)}, u32[]{:S(2)}, u32[]{:S(2)}) collective-permute-start(bf16[8,1024]{1,0:T(8,128)(2,1)} %vec.3), channel_id=1, source_target_pairs={{0,1},{1,0},{2,3},{3,2},{4,5},{5,4},{6,7},{7,6},{8,9},{9,8},{10,11... | collective-permute-start | bytes 49160 | tf_op jit(solution)/shard_map/ppermute | solution.py:296
  21.9 11.0 %all-to-all-start.1 = ((f32[32,1,128]{2,1,0:T(1,128)}), f32[32,1,128]{2,1,0:T(1,128)S(1)}, u32[]{:S(2)}, u32[]{:S(2)}) async-start(f32[32,1,128]{2,1,0:T(1,128)} %broadcast_in_dim.20), calls=%async_computation.1 | async-start | bytes 32768 | tf_op jit(solution)/shard_map/all_to_all | solution.py:317
  25.8 3.8 %collective-permute-start.2 = (bf16[8,1024]{1,0:T(8,128)(2,1)S(1)}, bf16[8,1024]{1,0:T(8,128)(2,1)S(1)}, u32[]{:S(2)}, u32[]{:S(2)}) collective-permute-start(bf16[8,1024]{1,0:T(8,128)(2,1)S(1)} %bitcast.4), channel_id=1, source_target_pairs={{0,1},{1,0},{2,3},{3,2},{4,5},{5,4},{6,7},{7,6},{8,9},{9,8},{10,11... | collective-permute-start | bytes 49160 | tf_op jit(solution)/shard_map/ppermute | solution.py:310

commit v2 on v1

--- a/solution.py
+++ b/solution.py
@@ -303,6 +303,8 @@
     copies = jnp.broadcast_to(vectors[None], (lax.axis_size("far"), kvec, own))
     gath = lax.all_to_all(copies, "far", 0, 0)
     gath = from_all(gath, "core")
+    late, gath[-1] = lax.optimization_barrier((vectors, gath[-1]))
+    others = from_all(late, "col")[1:]
     base, send, rest = tile_work(
         tile_rows, tile_cols, tile_count, gath, n_col, energies[None, :], tiles
     )
@@ -310,7 +312,6 @@
         lax.ppermute(send[s - 1], "col", [(c, (c + s) % n_col) for c in range(n_col)])
         for s in range(1, n_col)
     ]
-    others = from_all(vectors, "col")[1:]
     members = lax.axis_size(("far", "core", "col"))
     terms = gram_terms(base, rest, vectors, others)
     terms = jnp.broadcast_to(terms[None], (members,) + terms.shape)

time: 34 us -> 35.3 us (1.038)
  waiting for transfers between devices: 5.29 us -> 6.64 us
  starting transfers between devices: 7.25 us -> 6.89 us
    ppermute x2, waiting for transfers between devices: 0.01 us -> 1.35 us  [from_all(): lax.ppermute(x, axis, [(i, (i + s) % size) for i in range(size)])]
    all_to_all x1, starting transfers between devices: 3.89 us -> 3.53 us  [per_device(): gram_parts = lax.all_to_all(terms, ('far', 'core', 'col'), 0, 0)]
  transfers between devices with their start and end apart: 4 -> 4, of which waited for: 2 -> 3; matrix products, arithmetic and copies ran while one was open for 0% -> 0% of each run, Pallas kernels for 9% -> 8%
where the time goes in v2:
time: 35.3 us; the launch traced here: 34.7 us
  blocking collectives  14.4 us (41%)
  starting transfers between devices  6.89 us (20%)
  waiting for transfers between devices  6.64 us (19%)
  Pallas kernels  4 us (11%)
  local copies, waits for them, and re-layouts  1.43 us (4%)
  between operations  1.33 us (4%)
    all_to_all x1, blocking collectives, per_device(): gath = lax.all_to_all(copies, 'far', 0, 0)  14.4 us
    all_to_all x1, starting transfers between devices, per_device(): gram_parts = lax.all_to_all(terms, ('far', 'core', 'col'), 0, 0)  3.53 us
    all_to_all x1, waiting for transfers between devices, per_device(): gram_parts = lax.all_to_all(terms, ('far', 'core', 'col'), 0, 0)  3.3 us
    pallas_call x1, Pallas kernels, tile_work(): pl.pallas_call(functools.partial(tile_kernel, n_core, n_col, side), out_s...  2.94 us
    ppermute x1, waiting for transfers between devices, per_device(): lax.ppermute(send[s - 1], 'col', [(c, (c + s) % n_col) for c in range(n_c...  1.99 us
    ppermute x1, starting transfers between devices, per_device(): lax.ppermute(send[s - 1], 'col', [(c, (c + s) % n_col) for c in range(n_c...  1.83 us
    ppermute x2, starting transfers between devices, from_all(): lax.ppermute(x, axis, [(i, (i + s) % size) for i in range(size)])  1.52 us
    ppermute x2, waiting for transfers between devices, from_all(): lax.ppermute(x, axis, [(i, (i + s) % size) for i in range(size)])  1.35 us
  transfers between devices with their start and end apart: 4, of which 3 were waited for; matrix products, arithmetic and copies ran while one was open for 0% of the time, Pallas kernels for 8%

profile of v2, /device:TPU:0, one launch (start us, length us, event | category | flops | bytes accessed | tf_op | source)
XLA Modules:
  0.0 34.7 jit_solution(10419679109000823271)
XLA Ops:
  0.6 0.0 copy-start
  0.6 0.8 %broadcast_in_dim.18 = bf16[8,8,1024]{2,1,0:T(8,128)(2,1)S(1)} broadcast(bf16[8,1024]{1,0:T(8,128)(2,1)} %vec.3), dimensions={1,2} | broadcast | bytes 147456 | tf_op jit(solution)/shard_map/broadcast_in_dim | solution.py:303
  1.4 14.4 %all_to_all.10.refs_0_ = bf16[8,8,1024]{2,1,0:T(8,128)(2,1)S(1)} all-to-all(bf16[8,8,1024]{2,1,0:T(8,128)(2,1)S(1)} %broadcast_in_dim.18), channel_id=1, replica_groups=mesh['far'=8,'core'=2,'col'=2] {'far'}, dimensions={0} | all-to-all | bytes 262144 | tf_op jit(solution)/shard_map/all_to_all | solution.py:304
  15.8 0.0 collective-permute-start
  15.8 1.3 %collective-permute-done.refs_1_ = bf16[8,8,1024]{2,1,0:T(8,128)(2,1)S(1)} collective-permute-done((bf16[8,8,1024]{2,1,0:T(8,128)(2,1)S(1)}, bf16[8,8,1024]{2,1,0:T(8,128)(2,1)S(1)}, u32[]{:S(2)}, u32[]{:S(2)}) %collective-permute-start) | collective-permute-done | bytes 131104 | tf_op jit(solution)/shard_map/ppermute | solution.py:296
  17.2 1.5 %collective-permute-start.1 = (bf16[8,1024]{1,0:T(8,128)(2,1)}, bf16[8,1024]{1,0:T(8,128)(2,1)S(1)}, u32[]{:S(2)}, u32[]{:S(2)}) collective-permute-start(bf16[8,1024]{1,0:T(8,128)(2,1)} %vec.3), channel_id=1, source_target_pairs={{0,1},{1,0},{2,3},{3,2},{4,5},{5,4},{6,7},{7,6},{8,9},{9,8},{10,11... | collective-permute-start | bytes 49160 | tf_op jit(solution)/shard_map/ppermute | solution.py:296
  19.3 2.9 %tile_work.1 = (f32[8,1024]{1,0:T(8,128)S(1)}, bf16[1,8,1024]{2,1,0:T(8,128)(2,1)S(1)}, f32[1,8,1024]{2,1,0:T(8,128)S(1)}) custom-call(s32[1]{0:T(128)S(6)} %copy.8.count_s, s32[1024]{0:T(1024)} %rows_h.1, s32[1024]{0:T(1024)} %cols_h.1, f32[1,1024]{1,0:T(1,128)} %bitcast.5, bf16[1024,4096]{1,0:T(8,128)(2,1)} %tiles.1, ...), custom_call_target="tpu_custom_call" | custom-call | flops 67108864 | bytes 8388608 | tf_op jit(solution)/shard_map/tile_work/pallas_call | solution.py:194
  22.3 0.0 collective-permute-done.1.refs_0_
  22.3 0.0 copy-done
  22.3 0.3 gram_terms.1
  22.6 0.6 %broadcast_in_dim.20 = f32[32,1,128]{2,1,0:T(1,128)} broadcast(f32[128]{0:T(128)S(1)} %bitcast.3), dimensions={2} | broadcast | bytes 16896 | tf_op jit(solution)/shard_map/broadcast_in_dim | solution.py:317
  23.3 3.5 %all-to-all-start.1 = ((f32[32,1,128]{2,1,0:T(1,128)}), f32[32,1,128]{2,1,0:T(1,128)S(1)}, u32[]{:S(2)}, u32[]{:S(2)}) async-start(f32[32,1,128]{2,1,0:T(1,128)} %broadcast_in_dim.20), calls=%async_computation.1 | async-start | bytes 32768 | tf_op jit(solution)/shard_map/all_to_all | solution.py:318
  26.8 1.8 %collective-permute-start.2 = (bf16[8,1024]{1,0:T(8,128)(2,1)S(1)}, bf16[8,1024]{1,0:T(8,128)(2,1)S(1)}, u32[]{:S(2)}, u32[]{:S(2)}) collective-permute-start(bf16[8,1024]{1,0:T(8,128)(2,1)S(1)} %bitcast.4), channel_id=1, source_target_pairs={{0,1},{1,0},{2,3},{3,2},{4,5},{5,4},{6,7},{7,6},{8,9},{9,8},{10,11... | collective-permute-start | bytes 49160 | tf_op jit(solution)/shard_map/ppermute | solution.py:312
  28.6 2.0 %collective-permute-done.2.refs_0_ = bf16[8,1024]{1,0:T(8,128)(2,1)S(1)} collective-permute-done((bf16[8,1024]{1,0:T(8,128)(2,1)S(1)}, bf16[8,1024]{1,0:T(8,128)(2,1)S(1)}, u32[]{:S(2)}, u32[]{:S(2)}) %collective-permute-start.2) | collective-permute-done | bytes 16416 | tf_op jit(solution)/shard_map/ppermute | solution.py:312
  30.6 3.3 %all-to-all-done.1.gram_parts = f32[32,1,128]{2,1,0:T(1,128)S(1)} async-done(((f32[32,1,128]{2,1,0:T(1,128)}), f32[32,1,128]{2,1,0:T(1,128)S(1)}, u32[]{:S(2)}, u32[]{:S(2)}) %all-to-all-start.1) | async-done | bytes 16416 | tf_op jit(solution)/shard_map/all_to_all | solution.py:318
  33.9 0.8 %finish.1 = (bf16[8,1024]{1,0:T(8,128)(2,1)}, f32[8,1024]{1,0:T(8,128)}) custom-call(f32[8,1024]{1,0:T(8,128)S(1)} %get-tuple-element.8.own.base, f32[32,1,128]{2,1,0:T(1,128)S(1)} %all-to-all-done.1.gram_parts, bf16[8,1024]{1,0:T(8,128)(2,1)S(1)} %copy-done, bf16[8,1024]{1,0:T(8,128)(2,1)S(1)} %collective-permute-done.2.refs_0_), custom_call_target="tpu_custom_call" | custom-call | tf_op jit(solution)/shard_map/finish/pallas_call | solution.py:279
Async XLA Ops:
  0.6 21.7 %copy-start = (bf16[8,1024]{1,0:T(8,128)(2,1)S(1)}, bf16[8,1024]{1,0:T(8,128)(2,1)}, u32[]{:S(2)}) copy-start(bf16[8,1024]{1,0:T(8,128)(2,1)} %vec.3) | copy-start | bytes 49156
  15.8 1.3 %collective-permute-start = (bf16[8,8,1024]{2,1,0:T(8,128)(2,1)S(1)}, bf16[8,8,1024]{2,1,0:T(8,128)(2,1)S(1)}, u32[]{:S(2)}, u32[]{:S(2)}) collective-permute-start(bf16[8,8,1024]{2,1,0:T(8,128)(2,1)S(1)} %all_to_all.10.refs_0_), channel_id=1, source_target_pairs={{0,2},{2,0},{1,3},{3,1},{4,6},{6,4},{5,7},{7,5},{8,10},{10,8},{9,1... | collective-permute-start | bytes 393224 | tf_op jit(solution)/shard_map/ppermute | solution.py:296
  17.2 5.1 %collective-permute-start.1 = (bf16[8,1024]{1,0:T(8,128)(2,1)}, bf16[8,1024]{1,0:T(8,128)(2,1)S(1)}, u32[]{:S(2)}, u32[]{:S(2)}) collective-permute-start(bf16[8,1024]{1,0:T(8,128)(2,1)} %vec.3), channel_id=1, source_target_pairs={{0,1},{1,0},{2,3},{3,2},{4,5},{5,4},{6,7},{7,6},{8,9},{9,8},{10,11... | collective-permute-start | bytes 49160 | tf_op jit(solution)/shard_map/ppermute | solution.py:296
  23.3 10.7 %all-to-all-start.1 = ((f32[32,1,128]{2,1,0:T(1,128)}), f32[32,1,128]{2,1,0:T(1,128)S(1)}, u32[]{:S(2)}, u32[]{:S(2)}) async-start(f32[32,1,128]{2,1,0:T(1,128)} %broadcast_in_dim.20), calls=%async_computation.1 | async-start | bytes 32768 | tf_op jit(solution)/shard_map/all_to_all | solution.py:318
  26.8 3.8 %collective-permute-start.2 = (bf16[8,1024]{1,0:T(8,128)(2,1)S(1)}, bf16[8,1024]{1,0:T(8,128)(2,1)S(1)}, u32[]{:S(2)}, u32[]{:S(2)}) collective-permute-start(bf16[8,1024]{1,0:T(8,128)(2,1)S(1)} %bitcast.4), channel_id=1, source_target_pairs={{0,1},{1,0},{2,3},{3,2},{4,5},{5,4},{6,7},{7,6},{8,9},{9,8},{10,11... | collective-permute-start | bytes 49160 | tf_op jit(solution)/shard_map/ppermute | solution.py:312

commit v3 on v1

--- a/solution.py
+++ b/solution.py
@@ -131,21 +131,27 @@
 
     def full_step(i, carry):
         for ch in range(ahead):
-            ask((i + 2) * ahead + ch)
-        step(i * STEP, STEP, False)
+            ask(1 + (i + 2) * ahead + ch)
+        step(CHUNK + i * STEP, STEP, False)
         return carry
 
     def last_step(ch, carry):
         step(ch * CHUNK, CHUNK, True)
         return carry
 
-    for ch in range(ahead, 2 * ahead):
+    for ch in range(ahead, 1 + 2 * ahead):
         ask(ch)
     for copy in copies[:2]:
         copy.wait()
-    full = count // STEP
+    head = (count >= CHUNK).astype(jnp.int32)
+
+    @pl.when(head == 1)
+    def _():
+        step(0, CHUNK, False)
+
+    full = jnp.maximum(count - CHUNK, 0) // STEP
     lax.fori_loop(0, full, full_step, 0)
-    lax.fori_loop(full * (STEP // CHUNK), used, last_step, 0)
+    lax.fori_loop(head + full * ahead, used, last_step, 0)
 
     pairs = n_seg // per
 

time: 34 us -> 34.1 us (level)
  Pallas kernels: 4.01 us -> 5.04 us
  starting transfers between devices: 7.25 us -> 6.63 us
    pallas_call x1, Pallas kernels: 2.94 us -> 3.98 us  [tile_work(): pl.pallas_call(functools.partial(tile_kernel, n_core, n_col, side), out_s...]
    all_to_all x1, starting transfers between devices: 3.89 us -> 3.27 us  [per_device(): gram_parts = lax.all_to_all(terms, ('far', 'core', 'col'), 0, 0)]
  transfers between devices with their start and end apart: 4 -> 4, of which waited for: 2 -> 2; matrix products, arithmetic and copies ran while one was open for 0% -> 0% of each run, Pallas kernels for 9% -> 12%
where the time goes in v3:
time: 34.1 us
  blocking collectives  14.4 us (42%)
  starting transfers between devices  6.63 us (19%)
  waiting for transfers between devices  5.29 us (16%)
  Pallas kernels  5.04 us (15%)
  local copies, waits for them, and re-layouts  1.43 us (4%)
  between operations  1.33 us (4%)
    all_to_all x1, blocking collectives, per_device(): gath = lax.all_to_all(copies, 'far', 0, 0)  14.4 us
    pallas_call x1, Pallas kernels, tile_work(): pl.pallas_call(functools.partial(tile_kernel, n_core, n_col, side), out_s...  3.98 us
    all_to_all x1, waiting for transfers between devices, per_device(): gram_parts = lax.all_to_all(terms, ('far', 'core', 'col'), 0, 0)  3.3 us
    all_to_all x1, starting transfers between devices, per_device(): gram_parts = lax.all_to_all(terms, ('far', 'core', 'col'), 0, 0)  3.27 us
    ppermute x1, waiting for transfers between devices, per_device(): lax.ppermute(send[s - 1], 'col', [(c, (c + s) % n_col) for c in range(n_c...  1.99 us
    ppermute x1, starting transfers between devices, per_device(): lax.ppermute(send[s - 1], 'col', [(c, (c + s) % n_col) for c in range(n_c...  1.83 us
    ppermute x2, starting transfers between devices, from_all(): lax.ppermute(x, axis, [(i, (i + s) % size) for i in range(size)])  1.52 us
    broadcast_in_dim x1, local copies, waits for them, and re-layouts, per_device(): copies = jnp.broadcast_to(vectors[None], (lax.axis_size('far'), kvec, own))  0.79 us
  transfers between devices with their start and end apart: 4, of which 2 were waited for; matrix products, arithmetic and copies ran while one was open for 0% of the time, Pallas kernels for 12%

profile of v3, /device:TPU:0, one launch (start us, length us, event | category | flops | bytes accessed | tf_op | source)
XLA Modules:
  0.0 34.1 jit_solution(15381764234325673186)
XLA Ops:
  0.6 0.0 copy-start
  0.6 0.8 %broadcast_in_dim.18 = bf16[8,8,1024]{2,1,0:T(8,128)(2,1)S(1)} broadcast(bf16[8,1024]{1,0:T(8,128)(2,1)} %vec.3), dimensions={1,2} | broadcast | bytes 147456 | tf_op jit(solution)/shard_map/broadcast_in_dim | solution.py:309
  1.4 14.4 %all_to_all.10.refs_0_ = bf16[8,8,1024]{2,1,0:T(8,128)(2,1)S(1)} all-to-all(bf16[8,8,1024]{2,1,0:T(8,128)(2,1)S(1)} %broadcast_in_dim.18), channel_id=1, replica_groups=mesh['far'=8,'core'=2,'col'=2] {'far'}, dimensions={0} | all-to-all | bytes 262144 | tf_op jit(solution)/shard_map/all_to_all | solution.py:310
  15.8 0.0 collective-permute-start
  15.8 1.5 %collective-permute-start.1 = (bf16[8,1024]{1,0:T(8,128)(2,1)}, bf16[8,1024]{1,0:T(8,128)(2,1)S(1)}, u32[]{:S(2)}, u32[]{:S(2)}) collective-permute-start(bf16[8,1024]{1,0:T(8,128)(2,1)} %vec.3), channel_id=1, source_target_pairs={{0,1},{1,0},{2,3},{3,2},{4,5},{5,4},{6,7},{7,6},{8,9},{9,8},{10,11... | collective-permute-start | bytes 49160 | tf_op jit(solution)/shard_map/ppermute | solution.py:302
  18.0 0.0 collective-permute-done.refs_1_
  18.0 4.0 %tile_work.1 = (f32[8,1024]{1,0:T(8,128)S(1)}, bf16[1,8,1024]{2,1,0:T(8,128)(2,1)S(1)}, f32[1,8,1024]{2,1,0:T(8,128)S(1)}) custom-call(s32[1]{0:T(128)S(6)} %copy.8.count_s, s32[1024]{0:T(1024)} %rows_h.1, s32[1024]{0:T(1024)} %cols_h.1, f32[1,1024]{1,0:T(1,128)} %bitcast.5, bf16[1024,4096]{1,0:T(8,128)(2,1)} %tiles.1, ...), custom_call_target="tpu_custom_call" | custom-call | flops 67108864 | bytes 8388608 | tf_op jit(solution)/shard_map/tile_work/pallas_call | solution.py:200
  22.0 0.0 collective-permute-done.1.refs_0_
  22.0 0.0 copy-done
  22.0 0.3 gram_terms.1
  22.3 0.6 %broadcast_in_dim.20 = f32[32,1,128]{2,1,0:T(1,128)} broadcast(f32[128]{0:T(128)S(1)} %bitcast.3), dimensions={2} | broadcast | bytes 16896 | tf_op jit(solution)/shard_map/broadcast_in_dim | solution.py:322
  23.0 3.3 %all-to-all-start.1 = ((f32[32,1,128]{2,1,0:T(1,128)}), f32[32,1,128]{2,1,0:T(1,128)S(1)}, u32[]{:S(2)}, u32[]{:S(2)}) async-start(f32[32,1,128]{2,1,0:T(1,128)} %broadcast_in_dim.20), calls=%async_computation.1 | async-start | bytes 32768 | tf_op jit(solution)/shard_map/all_to_all | solution.py:323
  26.2 1.8 %collective-permute-start.2 = (bf16[8,1024]{1,0:T(8,128)(2,1)S(1)}, bf16[8,1024]{1,0:T(8,128)(2,1)S(1)}, u32[]{:S(2)}, u32[]{:S(2)}) collective-permute-start(bf16[8,1024]{1,0:T(8,128)(2,1)S(1)} %bitcast.4), channel_id=1, source_target_pairs={{0,1},{1,0},{2,3},{3,2},{4,5},{5,4},{6,7},{7,6},{8,9},{9,8},{10,11... | collective-permute-start | bytes 49160 | tf_op jit(solution)/shard_map/ppermute | solution.py:316
  28.1 2.0 %collective-permute-done.2.refs_0_ = bf16[8,1024]{1,0:T(8,128)(2,1)S(1)} collective-permute-done((bf16[8,1024]{1,0:T(8,128)(2,1)S(1)}, bf16[8,1024]{1,0:T(8,128)(2,1)S(1)}, u32[]{:S(2)}, u32[]{:S(2)}) %collective-permute-start.2) | collective-permute-done | bytes 16416 | tf_op jit(solution)/shard_map/ppermute | solution.py:316
  30.1 3.3 %all-to-all-done.1.gram_parts = f32[32,1,128]{2,1,0:T(1,128)S(1)} async-done(((f32[32,1,128]{2,1,0:T(1,128)}), f32[32,1,128]{2,1,0:T(1,128)S(1)}, u32[]{:S(2)}, u32[]{:S(2)}) %all-to-all-start.1) | async-done | bytes 16416 | tf_op jit(solution)/shard_map/all_to_all | solution.py:323
  33.4 0.8 %finish.1 = (bf16[8,1024]{1,0:T(8,128)(2,1)}, f32[8,1024]{1,0:T(8,128)}) custom-call(f32[8,1024]{1,0:T(8,128)S(1)} %get-tuple-element.5.own.base, f32[32,1,128]{2,1,0:T(1,128)S(1)} %all-to-all-done.1.gram_parts, bf16[8,1024]{1,0:T(8,128)(2,1)S(1)} %copy-done, bf16[8,1024]{1,0:T(8,128)(2,1)S(1)} %collective-permute-done.2.refs_0_), custom_call_target="tpu_custom_call" | custom-call | tf_op jit(solution)/shard_map/finish/pallas_call | solution.py:285
Async XLA Ops:
  0.6 21.4 %copy-start = (bf16[8,1024]{1,0:T(8,128)(2,1)S(1)}, bf16[8,1024]{1,0:T(8,128)(2,1)}, u32[]{:S(2)}) copy-start(bf16[8,1024]{1,0:T(8,128)(2,1)} %vec.3) | copy-start | bytes 49156
  15.8 2.2 %collective-permute-start = (bf16[8,8,1024]{2,1,0:T(8,128)(2,1)S(1)}, bf16[8,8,1024]{2,1,0:T(8,128)(2,1)S(1)}, u32[]{:S(2)}, u32[]{:S(2)}) collective-permute-start(bf16[8,8,1024]{2,1,0:T(8,128)(2,1)S(1)} %all_to_all.10.refs_0_), channel_id=1, source_target_pairs={{0,2},{2,0},{1,3},{3,1},{4,6},{6,4},{5,7},{7,5},{8,10},{10,8},{9,1... | collective-permute-start | bytes 393224 | tf_op jit(solution)/shard_map/ppermute | solution.py:302
  15.8 6.2 %collective-permute-start.1 = (bf16[8,1024]{1,0:T(8,128)(2,1)}, bf16[8,1024]{1,0:T(8,128)(2,1)S(1)}, u32[]{:S(2)}, u32[]{:S(2)}) collective-permute-start(bf16[8,1024]{1,0:T(8,128)(2,1)} %vec.3), channel_id=1, source_target_pairs={{0,1},{1,0},{2,3},{3,2},{4,5},{5,4},{6,7},{7,6},{8,9},{9,8},{10,11... | collective-permute-start | bytes 49160 | tf_op jit(solution)/shard_map/ppermute | solution.py:302
  23.0 10.4 %all-to-all-start.1 = ((f32[32,1,128]{2,1,0:T(1,128)}), f32[32,1,128]{2,1,0:T(1,128)S(1)}, u32[]{:S(2)}, u32[]{:S(2)}) async-start(f32[32,1,128]{2,1,0:T(1,128)} %broadcast_in_dim.20), calls=%async_computation.1 | async-start | bytes 32768 | tf_op jit(solution)/shard_map/all_to_all | solution.py:323
  26.2 3.8 %collective-permute-start.2 = (bf16[8,1024]{1,0:T(8,128)(2,1)S(1)}, bf16[8,1024]{1,0:T(8,128)(2,1)S(1)}, u32[]{:S(2)}, u32[]{:S(2)}) collective-permute-start(bf16[8,1024]{1,0:T(8,128)(2,1)S(1)} %bitcast.4), channel_id=1, source_target_pairs={{0,1},{1,0},{2,3},{3,2},{4,5},{5,4},{6,7},{7,6},{8,9},{9,8},{10,11... | collective-permute-start | bytes 49160 | tf_op jit(solution)/shard_map/ppermute | solution.py:316

commit v4 on v3

--- a/solution.py
+++ b/solution.py
@@ -94,9 +94,7 @@
 
     def product(base, half, x, check):
         xh = x[half * SUB:(half + 1) * SUB]
-        w = jnp.concatenate(
-            [xh[:, c * LANES:(c + 1) * LANES] for c in range(n_chunk)], axis=0
-        ).astype(jnp.bfloat16)
+        w = jnp.concatenate([xh[:, c * LANES:(c + 1) * LANES] for c in range(n_chunk)], axis=0)
         entries = []
         for t in range(SUB):
             slot = base + half * SUB + t
@@ -121,7 +119,7 @@
         waiting = None
         for q in range(slots_in // (2 * SUB)):
             base = pl.multiple_of(first + q * 2 * SUB, 2 * SUB)
-            x = buf[pl.ds(base, 2 * SUB), :].astype(jnp.float32)
+            x = buf[pl.ds(base, 2 * SUB), :]
             for half in range(2):
                 out = product(base, half, x, check)
                 if waiting is not None:

time: 34.1 us -> 34 us (level); the launches traced: 34.1 us -> 33.7 us
  Pallas kernels: 5.04 us -> 4.5 us
    pallas_call x1, Pallas kernels: 3.98 us -> 3.44 us  [tile_work(): pl.pallas_call(functools.partial(tile_kernel, n_core, n_col, side), out_s...]
  transfers between devices with their start and end apart: 4 -> 4, of which waited for: 2 -> 2; matrix products, arithmetic and copies ran while one was open for 0% -> 0% of each run, Pallas kernels for 12% -> 10%
where the time goes in v4:
time: 34 us; the launch traced here: 33.7 us
  blocking collectives  14.4 us (42%)
  starting transfers between devices  6.87 us (20%)
  waiting for transfers between devices  5.14 us (15%)
  Pallas kernels  4.5 us (13%)
  local copies, waits for them, and re-layouts  1.43 us (4%)
  between operations  1.33 us (4%)
    all_to_all x1, blocking collectives, per_device(): gath = lax.all_to_all(copies, 'far', 0, 0)  14.4 us
    pallas_call x1, Pallas kernels, tile_work(): pl.pallas_call(functools.partial(tile_kernel, n_core, n_col, side), out_s...  3.44 us
    all_to_all x1, starting transfers between devices, per_device(): gram_parts = lax.all_to_all(terms, ('far', 'core', 'col'), 0, 0)  3.36 us
    all_to_all x1, waiting for transfers between devices, per_device(): gram_parts = lax.all_to_all(terms, ('far', 'core', 'col'), 0, 0)  3.3 us
    ppermute x1, starting transfers between devices, per_device(): lax.ppermute(send[s - 1], 'col', [(c, (c + s) % n_col) for c in range(n_c...  1.99 us
    ppermute x1, waiting for transfers between devices, per_device(): lax.ppermute(send[s - 1], 'col', [(c, (c + s) % n_col) for c in range(n_c...  1.84 us
    ppermute x2, starting transfers between devices, from_all(): lax.ppermute(x, axis, [(i, (i + s) % size) for i in range(size)])  1.52 us
    broadcast_in_dim x1, local copies, waits for them, and re-layouts, per_device(): copies = jnp.broadcast_to(vectors[None], (lax.axis_size('far'), kvec, own))  0.79 us
  transfers between devices with their start and end apart: 4, of which 2 were waited for; matrix products, arithmetic and copies ran while one was open for 0% of the time, Pallas kernels for 10%

profile of v4, /device:TPU:0, one launch (start us, length us, event | category | flops | bytes accessed | tf_op | source)
XLA Modules:
  0.0 33.7 jit_solution(5749115684188865290)
XLA Ops:
  0.6 0.0 copy-start
  0.6 0.8 %broadcast_in_dim.18 = bf16[8,8,1024]{2,1,0:T(8,128)(2,1)S(1)} broadcast(bf16[8,1024]{1,0:T(8,128)(2,1)} %vec.3), dimensions={1,2} | broadcast | bytes 147456 | tf_op jit(solution)/shard_map/broadcast_in_dim | solution.py:307
  1.4 14.4 %all_to_all.10.refs_0_ = bf16[8,8,1024]{2,1,0:T(8,128)(2,1)S(1)} all-to-all(bf16[8,8,1024]{2,1,0:T(8,128)(2,1)S(1)} %broadcast_in_dim.18), channel_id=1, replica_groups=mesh['far'=8,'core'=2,'col'=2] {'far'}, dimensions={0} | all-to-all | bytes 262144 | tf_op jit(solution)/shard_map/all_to_all | solution.py:308
  15.8 0.0 collective-permute-start
  15.8 1.5 %collective-permute-start.1 = (bf16[8,1024]{1,0:T(8,128)(2,1)}, bf16[8,1024]{1,0:T(8,128)(2,1)S(1)}, u32[]{:S(2)}, u32[]{:S(2)}) collective-permute-start(bf16[8,1024]{1,0:T(8,128)(2,1)} %vec.3), channel_id=1, source_target_pairs={{0,1},{1,0},{2,3},{3,2},{4,5},{5,4},{6,7},{7,6},{8,9},{9,8},{10,11... | collective-permute-start | bytes 49160 | tf_op jit(solution)/shard_map/ppermute | solution.py:300
  18.0 0.0 collective-permute-done.refs_1_
  18.0 3.4 %tile_work.1 = (f32[8,1024]{1,0:T(8,128)S(1)}, bf16[1,8,1024]{2,1,0:T(8,128)(2,1)S(1)}, f32[1,8,1024]{2,1,0:T(8,128)S(1)}) custom-call(s32[1]{0:T(128)S(6)} %copy.8.count_s, s32[1024]{0:T(1024)} %rows_h.1, s32[1024]{0:T(1024)} %cols_h.1, f32[1,1024]{1,0:T(1,128)} %bitcast.5, bf16[1024,4096]{1,0:T(8,128)(2,1)} %tiles.1, ...), custom_call_target="tpu_custom_call" | custom-call | flops 67108864 | bytes 8388608 | tf_op jit(solution)/shard_map/tile_work/pallas_call | solution.py:198
  21.5 0.0 collective-permute-done.1.refs_0_
  21.5 0.0 copy-done
  21.5 0.3 gram_terms.1
  21.8 0.6 %broadcast_in_dim.20 = f32[32,1,128]{2,1,0:T(1,128)} broadcast(f32[128]{0:T(128)S(1)} %bitcast.3), dimensions={2} | broadcast | bytes 16896 | tf_op jit(solution)/shard_map/broadcast_in_dim | solution.py:320
  22.4 3.4 %all-to-all-start.1 = ((f32[32,1,128]{2,1,0:T(1,128)}), f32[32,1,128]{2,1,0:T(1,128)S(1)}, u32[]{:S(2)}, u32[]{:S(2)}) async-start(f32[32,1,128]{2,1,0:T(1,128)} %broadcast_in_dim.20), calls=%async_computation.1 | async-start | bytes 32768 | tf_op jit(solution)/shard_map/all_to_all | solution.py:321
  25.8 2.0 %collective-permute-start.2 = (bf16[8,1024]{1,0:T(8,128)(2,1)S(1)}, bf16[8,1024]{1,0:T(8,128)(2,1)S(1)}, u32[]{:S(2)}, u32[]{:S(2)}) collective-permute-start(bf16[8,1024]{1,0:T(8,128)(2,1)S(1)} %bitcast.4), channel_id=1, source_target_pairs={{0,1},{1,0},{2,3},{3,2},{4,5},{5,4},{6,7},{7,6},{8,9},{9,8},{10,11... | collective-permute-start | bytes 49160 | tf_op jit(solution)/shard_map/ppermute | solution.py:314
  27.8 1.8 %collective-permute-done.2.refs_0_ = bf16[8,1024]{1,0:T(8,128)(2,1)S(1)} collective-permute-done((bf16[8,1024]{1,0:T(8,128)(2,1)S(1)}, bf16[8,1024]{1,0:T(8,128)(2,1)S(1)}, u32[]{:S(2)}, u32[]{:S(2)}) %collective-permute-start.2) | collective-permute-done | bytes 16416 | tf_op jit(solution)/shard_map/ppermute | solution.py:314
  29.6 3.3 %all-to-all-done.1.gram_parts = f32[32,1,128]{2,1,0:T(1,128)S(1)} async-done(((f32[32,1,128]{2,1,0:T(1,128)}), f32[32,1,128]{2,1,0:T(1,128)S(1)}, u32[]{:S(2)}, u32[]{:S(2)}) %all-to-all-start.1) | async-done | bytes 16416 | tf_op jit(solution)/shard_map/all_to_all | solution.py:321
  32.9 0.8 %finish.1 = (bf16[8,1024]{1,0:T(8,128)(2,1)}, f32[8,1024]{1,0:T(8,128)}) custom-call(f32[8,1024]{1,0:T(8,128)S(1)} %get-tuple-element.5.own.base, f32[32,1,128]{2,1,0:T(1,128)S(1)} %all-to-all-done.1.gram_parts, bf16[8,1024]{1,0:T(8,128)(2,1)S(1)} %copy-done, bf16[8,1024]{1,0:T(8,128)(2,1)S(1)} %collective-permute-done.2.refs_0_), custom_call_target="tpu_custom_call" | custom-call | tf_op jit(solution)/shard_map/finish/pallas_call | solution.py:283
Async XLA Ops:
  0.6 20.8 %copy-start = (bf16[8,1024]{1,0:T(8,128)(2,1)S(1)}, bf16[8,1024]{1,0:T(8,128)(2,1)}, u32[]{:S(2)}) copy-start(bf16[8,1024]{1,0:T(8,128)(2,1)} %vec.3) | copy-start | bytes 49156
  15.8 2.2 %collective-permute-start = (bf16[8,8,1024]{2,1,0:T(8,128)(2,1)S(1)}, bf16[8,8,1024]{2,1,0:T(8,128)(2,1)S(1)}, u32[]{:S(2)}, u32[]{:S(2)}) collective-permute-start(bf16[8,8,1024]{2,1,0:T(8,128)(2,1)S(1)} %all_to_all.10.refs_0_), channel_id=1, source_target_pairs={{0,2},{2,0},{1,3},{3,1},{4,6},{6,4},{5,7},{7,5},{8,10},{10,8},{9,1... | collective-permute-start | bytes 393224 | tf_op jit(solution)/shard_map/ppermute | solution.py:300
  15.8 5.6 %collective-permute-start.1 = (bf16[8,1024]{1,0:T(8,128)(2,1)}, bf16[8,1024]{1,0:T(8,128)(2,1)S(1)}, u32[]{:S(2)}, u32[]{:S(2)}) collective-permute-start(bf16[8,1024]{1,0:T(8,128)(2,1)} %vec.3), channel_id=1, source_target_pairs={{0,1},{1,0},{2,3},{3,2},{4,5},{5,4},{6,7},{7,6},{8,9},{9,8},{10,11... | collective-permute-start | bytes 49160 | tf_op jit(solution)/shard_map/ppermute | solution.py:300
  22.4 10.5 %all-to-all-start.1 = ((f32[32,1,128]{2,1,0:T(1,128)}), f32[32,1,128]{2,1,0:T(1,128)S(1)}, u32[]{:S(2)}, u32[]{:S(2)}) async-start(f32[32,1,128]{2,1,0:T(1,128)} %broadcast_in_dim.20), calls=%async_computation.1 | async-start | bytes 32768 | tf_op jit(solution)/shard_map/all_to_all | solution.py:321
  25.8 3.8 %collective-permute-start.2 = (bf16[8,1024]{1,0:T(8,128)(2,1)S(1)}, bf16[8,1024]{1,0:T(8,128)(2,1)S(1)}, u32[]{:S(2)}, u32[]{:S(2)}) collective-permute-start(bf16[8,1024]{1,0:T(8,128)(2,1)S(1)} %bitcast.4), channel_id=1, source_target_pairs={{0,1},{1,0},{2,3},{3,2},{4,5},{5,4},{6,7},{7,6},{8,9},{9,8},{10,11... | collective-permute-start | bytes 49160 | tf_op jit(solution)/shard_map/ppermute | solution.py:314

commit v5 on v3

--- a/solution.py
+++ b/solution.py
@@ -320,7 +320,7 @@
     members = lax.axis_size(("far", "core", "col"))
     terms = gram_terms(base, rest, vectors, others)
     terms = jnp.broadcast_to(terms[None], (members,) + terms.shape)
-    gram_parts = lax.all_to_all(terms, ("far", "core", "col"), 0, 0)
+    gram_parts = lax.all_to_all(terms, ("col", "core", "far"), 0, 0)
     return finish(1.0 / (members * own), base, gram_parts, vectors, got)
 
 

time: 34.1 us -> 34.1 us (level); the launches traced: 34.1 us -> 33.5 us
  Pallas kernels: 5.04 us -> 4.48 us
    pallas_call x1, Pallas kernels: 3.98 us -> 3.41 us  [tile_work(): pl.pallas_call(functools.partial(tile_kernel, n_core, n_col, side), out_s...]
  transfers between devices with their start and end apart: 4 -> 4, of which waited for: 2 -> 2; matrix products, arithmetic and copies ran while one was open for 0% -> 0% of each run, Pallas kernels for 12% -> 10%
where the time goes in v5:
time: 34.1 us; the launch traced here: 33.5 us
  blocking collectives  14.4 us (42%)
  starting transfers between devices  6.83 us (20%)
  waiting for transfers between devices  5.06 us (15%)
  Pallas kernels  4.48 us (13%)
  local copies, waits for them, and re-layouts  1.43 us (4%)
  between operations  1.33 us (4%)
    all_to_all x1, blocking collectives, per_device(): gath = lax.all_to_all(copies, 'far', 0, 0)  14.4 us
    pallas_call x1, Pallas kernels, tile_work(): pl.pallas_call(functools.partial(tile_kernel, n_core, n_col, side), out_s...  3.41 us
    all_to_all x1, starting transfers between devices, per_device(): gram_parts = lax.all_to_all(terms, ('col', 'core', 'far'), 0, 0)  3.32 us
    all_to_all x1, waiting for transfers between devices, per_device(): gram_parts = lax.all_to_all(terms, ('col', 'core', 'far'), 0, 0)  3.21 us
    ppermute x1, starting transfers between devices, per_device(): lax.ppermute(send[s - 1], 'col', [(c, (c + s) % n_col) for c in range(n_c...  1.99 us
    ppermute x1, waiting for transfers between devices, per_device(): lax.ppermute(send[s - 1], 'col', [(c, (c + s) % n_col) for c in range(n_c...  1.84 us
    ppermute x2, starting transfers between devices, from_all(): lax.ppermute(x, axis, [(i, (i + s) % size) for i in range(size)])  1.52 us
    broadcast_in_dim x1, local copies, waits for them, and re-layouts, per_device(): copies = jnp.broadcast_to(vectors[None], (lax.axis_size('far'), kvec, own))  0.79 us
  transfers between devices with their start and end apart: 4, of which 2 were waited for; matrix products, arithmetic and copies ran while one was open for 0% of the time, Pallas kernels for 10%

profile of v5, /device:TPU:0, one launch (start us, length us, event | category | flops | bytes accessed | tf_op | source)
XLA Modules:
  0.0 33.5 jit_solution(4170008087712412931)
XLA Ops:
  0.6 0.0 copy-start
  0.6 0.8 %broadcast_in_dim.18 = bf16[8,8,1024]{2,1,0:T(8,128)(2,1)S(1)} broadcast(bf16[8,1024]{1,0:T(8,128)(2,1)} %vec.3), dimensions={1,2} | broadcast | bytes 147456 | tf_op jit(solution)/shard_map/broadcast_in_dim | solution.py:309
  1.4 14.4 %all_to_all.10.refs_0_ = bf16[8,8,1024]{2,1,0:T(8,128)(2,1)S(1)} all-to-all(bf16[8,8,1024]{2,1,0:T(8,128)(2,1)S(1)} %broadcast_in_dim.18), channel_id=1, replica_groups=mesh['far'=8,'core'=2,'col'=2] {'far'}, dimensions={0} | all-to-all | bytes 262144 | tf_op jit(solution)/shard_map/all_to_all | solution.py:310
  15.8 0.0 collective-permute-start
  15.8 1.5 %collective-permute-start.1 = (bf16[8,1024]{1,0:T(8,128)(2,1)}, bf16[8,1024]{1,0:T(8,128)(2,1)S(1)}, u32[]{:S(2)}, u32[]{:S(2)}) collective-permute-start(bf16[8,1024]{1,0:T(8,128)(2,1)} %vec.3), channel_id=1, source_target_pairs={{0,1},{1,0},{2,3},{3,2},{4,5},{5,4},{6,7},{7,6},{8,9},{9,8},{10,11... | collective-permute-start | bytes 49160 | tf_op jit(solution)/shard_map/ppermute | solution.py:302
  18.0 0.0 collective-permute-done.refs_1_
  18.0 3.4 %tile_work.1 = (f32[8,1024]{1,0:T(8,128)S(1)}, bf16[1,8,1024]{2,1,0:T(8,128)(2,1)S(1)}, f32[1,8,1024]{2,1,0:T(8,128)S(1)}) custom-call(s32[1]{0:T(128)S(6)} %copy.8.count_s, s32[1024]{0:T(1024)} %rows_h.1, s32[1024]{0:T(1024)} %cols_h.1, f32[1,1024]{1,0:T(1,128)} %bitcast.5, bf16[1024,4096]{1,0:T(8,128)(2,1)} %tiles.1, ...), custom_call_target="tpu_custom_call" | custom-call | flops 67108864 | bytes 8388608 | tf_op jit(solution)/shard_map/tile_work/pallas_call | solution.py:200
  21.4 0.0 collective-permute-done.1.refs_0_
  21.4 0.0 copy-done
  21.5 0.3 gram_terms.1
  21.8 0.6 %broadcast_in_dim.20 = f32[32,1,128]{2,1,0:T(1,128)} broadcast(f32[128]{0:T(128)S(1)} %bitcast.3), dimensions={2} | broadcast | bytes 16896 | tf_op jit(solution)/shard_map/broadcast_in_dim | solution.py:322
  22.4 3.3 %all-to-all-start.1 = ((f32[32,1,128]{2,1,0:T(1,128)}), f32[32,1,128]{2,1,0:T(1,128)S(1)}, u32[]{:S(2)}, u32[]{:S(2)}) async-start(f32[32,1,128]{2,1,0:T(1,128)} %broadcast_in_dim.20), calls=%async_computation.1 | async-start | bytes 32768 | tf_op jit(solution)/shard_map/all_to_all | solution.py:323
  25.7 2.0 %collective-permute-start.2 = (bf16[8,1024]{1,0:T(8,128)(2,1)S(1)}, bf16[8,1024]{1,0:T(8,128)(2,1)S(1)}, u32[]{:S(2)}, u32[]{:S(2)}) collective-permute-start(bf16[8,1024]{1,0:T(8,128)(2,1)S(1)} %bitcast.4), channel_id=1, source_target_pairs={{0,1},{1,0},{2,3},{3,2},{4,5},{5,4},{6,7},{7,6},{8,9},{9,8},{10,11... | collective-permute-start | bytes 49160 | tf_op jit(solution)/shard_map/ppermute | solution.py:316
  27.7 1.8 %collective-permute-done.2.refs_0_ = bf16[8,1024]{1,0:T(8,128)(2,1)S(1)} collective-permute-done((bf16[8,1024]{1,0:T(8,128)(2,1)S(1)}, bf16[8,1024]{1,0:T(8,128)(2,1)S(1)}, u32[]{:S(2)}, u32[]{:S(2)}) %collective-permute-start.2) | collective-permute-done | bytes 16416 | tf_op jit(solution)/shard_map/ppermute | solution.py:316
  29.6 3.2 %all-to-all-done.1.gram_parts = f32[32,1,128]{2,1,0:T(1,128)S(1)} async-done(((f32[32,1,128]{2,1,0:T(1,128)}), f32[32,1,128]{2,1,0:T(1,128)S(1)}, u32[]{:S(2)}, u32[]{:S(2)}) %all-to-all-start.1) | async-done | bytes 16416 | tf_op jit(solution)/shard_map/all_to_all | solution.py:323
  32.8 0.8 %finish.1 = (bf16[8,1024]{1,0:T(8,128)(2,1)}, f32[8,1024]{1,0:T(8,128)}) custom-call(f32[8,1024]{1,0:T(8,128)S(1)} %get-tuple-element.5.own.base, f32[32,1,128]{2,1,0:T(1,128)S(1)} %all-to-all-done.1.gram_parts, bf16[8,1024]{1,0:T(8,128)(2,1)S(1)} %copy-done, bf16[8,1024]{1,0:T(8,128)(2,1)S(1)} %collective-permute-done.2.refs_0_), custom_call_target="tpu_custom_call" | custom-call | tf_op jit(solution)/shard_map/finish/pallas_call | solution.py:285
Async XLA Ops:
  0.6 20.8 %copy-start = (bf16[8,1024]{1,0:T(8,128)(2,1)S(1)}, bf16[8,1024]{1,0:T(8,128)(2,1)}, u32[]{:S(2)}) copy-start(bf16[8,1024]{1,0:T(8,128)(2,1)} %vec.3) | copy-start | bytes 49156
  15.8 2.2 %collective-permute-start = (bf16[8,8,1024]{2,1,0:T(8,128)(2,1)S(1)}, bf16[8,8,1024]{2,1,0:T(8,128)(2,1)S(1)}, u32[]{:S(2)}, u32[]{:S(2)}) collective-permute-start(bf16[8,8,1024]{2,1,0:T(8,128)(2,1)S(1)} %all_to_all.10.refs_0_), channel_id=1, source_target_pairs={{0,2},{2,0},{1,3},{3,1},{4,6},{6,4},{5,7},{7,5},{8,10},{10,8},{9,1... | collective-permute-start | bytes 393224 | tf_op jit(solution)/shard_map/ppermute | solution.py:302
  15.8 5.6 %collective-permute-start.1 = (bf16[8,1024]{1,0:T(8,128)(2,1)}, bf16[8,1024]{1,0:T(8,128)(2,1)S(1)}, u32[]{:S(2)}, u32[]{:S(2)}) collective-permute-start(bf16[8,1024]{1,0:T(8,128)(2,1)} %vec.3), channel_id=1, source_target_pairs={{0,1},{1,0},{2,3},{3,2},{4,5},{5,4},{6,7},{7,6},{8,9},{9,8},{10,11... | collective-permute-start | bytes 49160 | tf_op jit(solution)/shard_map/ppermute | solution.py:302
  22.4 10.4 %all-to-all-start.1 = ((f32[32,1,128]{2,1,0:T(1,128)}), f32[32,1,128]{2,1,0:T(1,128)S(1)}, u32[]{:S(2)}, u32[]{:S(2)}) async-start(f32[32,1,128]{2,1,0:T(1,128)} %broadcast_in_dim.20), calls=%async_computation.1 | async-start | bytes 32768 | tf_op jit(solution)/shard_map/all_to_all | solution.py:323
  25.7 3.8 %collective-permute-start.2 = (bf16[8,1024]{1,0:T(8,128)(2,1)S(1)}, bf16[8,1024]{1,0:T(8,128)(2,1)S(1)}, u32[]{:S(2)}, u32[]{:S(2)}) collective-permute-start(bf16[8,1024]{1,0:T(8,128)(2,1)S(1)} %bitcast.4), channel_id=1, source_target_pairs={{0,1},{1,0},{2,3},{3,2},{4,5},{5,4},{6,7},{7,6},{8,9},{9,8},{10,11... | collective-permute-start | bytes 49160 | tf_op jit(solution)/shard_map/ppermute | solution.py:316

commit v6 on v3

--- a/solution.py
+++ b/solution.py
@@ -12,7 +12,7 @@
 SUB = 8
 CHUNK = 128
 STEP = 256
-SUMS = 4
+SUMS = 2
 
 NT = (((1,), (1,)), ((), ()))
 

time: 34.1 us -> 34.7 us (1.018)
  starting transfers between devices: 6.63 us -> 8.02 us
  Pallas kernels: 5.04 us -> 4.05 us
    all_to_all x1, starting transfers between devices: 3.27 us -> 4.66 us  [per_device(): gram_parts = lax.all_to_all(terms, ('far', 'core', 'col'), 0, 0)]
    pallas_call x1, Pallas kernels: 3.98 us -> 2.99 us  [tile_work(): pl.pallas_call(functools.partial(tile_kernel, n_core, n_col, side), out_s...]
  transfers between devices with their start and end apart: 4 -> 4, of which waited for: 2 -> 2; matrix products, arithmetic and copies ran while one was open for 0% -> 0% of each run, Pallas kernels for 12% -> 9%
where the time goes in v6:
time: 34.7 us; the launch traced here: 34.5 us
  blocking collectives  14.4 us (41%)
  starting transfers between devices  8.02 us (23%)
  waiting for transfers between devices  5.29 us (15%)
  Pallas kernels  4.05 us (12%)
  local copies, waits for them, and re-layouts  1.43 us (4%)
  between operations  1.33 us (4%)
    all_to_all x1, blocking collectives, per_device(): gath = lax.all_to_all(copies, 'far', 0, 0)  14.4 us
    all_to_all x1, starting transfers between devices, per_device(): gram_parts = lax.all_to_all(terms, ('far', 'core', 'col'), 0, 0)  4.66 us
    all_to_all x1, waiting for transfers between devices, per_device(): gram_parts = lax.all_to_all(terms, ('far', 'core', 'col'), 0, 0)  3.21 us
    pallas_call x1, Pallas kernels, tile_work(): pl.pallas_call(functools.partial(tile_kernel, n_core, n_col, side), out_s...  2.99 us
    ppermute x1, waiting for transfers between devices, per_device(): lax.ppermute(send[s - 1], 'col', [(c, (c + s) % n_col) for c in range(n_c...  2.08 us
    ppermute x1, starting transfers between devices, per_device(): lax.ppermute(send[s - 1], 'col', [(c, (c + s) % n_col) for c in range(n_c...  1.83 us
    ppermute x2, starting transfers between devices, from_all(): lax.ppermute(x, axis, [(i, (i + s) % size) for i in range(size)])  1.52 us
    broadcast_in_dim x1, local copies, waits for them, and re-layouts, per_device(): copies = jnp.broadcast_to(vectors[None], (lax.axis_size('far'), kvec, own))  0.79 us
  transfers between devices with their start and end apart: 4, of which 2 were waited for; matrix products, arithmetic and copies ran while one was open for 0% of the time, Pallas kernels for 9%

profile of v6, /device:TPU:0, one launch (start us, length us, event | category | flops | bytes accessed | tf_op | source)
XLA Modules:
  0.0 34.5 jit_solution(7817273668232713480)
XLA Ops:
  0.6 0.0 copy-start
  0.6 0.8 %broadcast_in_dim.18 = bf16[8,8,1024]{2,1,0:T(8,128)(2,1)S(1)} broadcast(bf16[8,1024]{1,0:T(8,128)(2,1)} %vec.3), dimensions={1,2} | broadcast | bytes 147456 | tf_op jit(solution)/shard_map/broadcast_in_dim | solution.py:309
  1.4 14.4 %all_to_all.10.refs_0_ = bf16[8,8,1024]{2,1,0:T(8,128)(2,1)S(1)} all-to-all(bf16[8,8,1024]{2,1,0:T(8,128)(2,1)S(1)} %broadcast_in_dim.18), channel_id=1, replica_groups=mesh['far'=8,'core'=2,'col'=2] {'far'}, dimensions={0} | all-to-all | bytes 262144 | tf_op jit(solution)/shard_map/all_to_all | solution.py:310
  15.8 0.0 collective-permute-start
  15.8 1.5 %collective-permute-start.1 = (bf16[8,1024]{1,0:T(8,128)(2,1)}, bf16[8,1024]{1,0:T(8,128)(2,1)S(1)}, u32[]{:S(2)}, u32[]{:S(2)}) collective-permute-start(bf16[8,1024]{1,0:T(8,128)(2,1)} %vec.3), channel_id=1, source_target_pairs={{0,1},{1,0},{2,3},{3,2},{4,5},{5,4},{6,7},{7,6},{8,9},{9,8},{10,11... | collective-permute-start | bytes 49160 | tf_op jit(solution)/shard_map/ppermute | solution.py:302
  18.0 0.0 collective-permute-done.refs_1_
  18.0 3.0 %tile_work.1 = (f32[8,1024]{1,0:T(8,128)S(1)}, bf16[1,8,1024]{2,1,0:T(8,128)(2,1)S(1)}, f32[1,8,1024]{2,1,0:T(8,128)S(1)}) custom-call(s32[1]{0:T(128)S(6)} %copy.8.count_s, s32[1024]{0:T(1024)} %rows_h.1, s32[1024]{0:T(1024)} %cols_h.1, f32[1,1024]{1,0:T(1,128)} %bitcast.5, bf16[1024,4096]{1,0:T(8,128)(2,1)} %tiles.1, ...), custom_call_target="tpu_custom_call" | custom-call | flops 67108864 | bytes 8388608 | tf_op jit(solution)/shard_map/tile_work/pallas_call | solution.py:200
  21.0 0.0 collective-permute-done.1.refs_0_
  21.0 0.0 copy-done
  21.0 0.3 gram_terms.1
  21.3 0.6 %broadcast_in_dim.20 = f32[32,1,128]{2,1,0:T(1,128)} broadcast(f32[128]{0:T(128)S(1)} %bitcast.3), dimensions={2} | broadcast | bytes 16896 | tf_op jit(solution)/shard_map/broadcast_in_dim | solution.py:322
  22.0 4.7 %all-to-all-start.1 = ((f32[32,1,128]{2,1,0:T(1,128)}), f32[32,1,128]{2,1,0:T(1,128)S(1)}, u32[]{:S(2)}, u32[]{:S(2)}) async-start(f32[32,1,128]{2,1,0:T(1,128)} %broadcast_in_dim.20), calls=%async_computation.1 | async-start | bytes 32768 | tf_op jit(solution)/shard_map/all_to_all | solution.py:323
  26.6 1.8 %collective-permute-start.2 = (bf16[8,1024]{1,0:T(8,128)(2,1)S(1)}, bf16[8,1024]{1,0:T(8,128)(2,1)S(1)}, u32[]{:S(2)}, u32[]{:S(2)}) collective-permute-start(bf16[8,1024]{1,0:T(8,128)(2,1)S(1)} %bitcast.4), channel_id=1, source_target_pairs={{0,1},{1,0},{2,3},{3,2},{4,5},{5,4},{6,7},{7,6},{8,9},{9,8},{10,11... | collective-permute-start | bytes 49160 | tf_op jit(solution)/shard_map/ppermute | solution.py:316
  28.5 2.1 %collective-permute-done.2.refs_0_ = bf16[8,1024]{1,0:T(8,128)(2,1)S(1)} collective-permute-done((bf16[8,1024]{1,0:T(8,128)(2,1)S(1)}, bf16[8,1024]{1,0:T(8,128)(2,1)S(1)}, u32[]{:S(2)}, u32[]{:S(2)}) %collective-permute-start.2) | collective-permute-done | bytes 16416 | tf_op jit(solution)/shard_map/ppermute | solution.py:316
  30.6 3.2 %all-to-all-done.1.gram_parts = f32[32,1,128]{2,1,0:T(1,128)S(1)} async-done(((f32[32,1,128]{2,1,0:T(1,128)}), f32[32,1,128]{2,1,0:T(1,128)S(1)}, u32[]{:S(2)}, u32[]{:S(2)}) %all-to-all-start.1) | async-done | bytes 16416 | tf_op jit(solution)/shard_map/all_to_all | solution.py:323
  33.8 0.8 %finish.1 = (bf16[8,1024]{1,0:T(8,128)(2,1)}, f32[8,1024]{1,0:T(8,128)}) custom-call(f32[8,1024]{1,0:T(8,128)S(1)} %get-tuple-element.5.own.base, f32[32,1,128]{2,1,0:T(1,128)S(1)} %all-to-all-done.1.gram_parts, bf16[8,1024]{1,0:T(8,128)(2,1)S(1)} %copy-done, bf16[8,1024]{1,0:T(8,128)(2,1)S(1)} %collective-permute-done.2.refs_0_), custom_call_target="tpu_custom_call" | custom-call | tf_op jit(solution)/shard_map/finish/pallas_call | solution.py:285
Async XLA Ops:
  0.6 20.4 %copy-start = (bf16[8,1024]{1,0:T(8,128)(2,1)S(1)}, bf16[8,1024]{1,0:T(8,128)(2,1)}, u32[]{:S(2)}) copy-start(bf16[8,1024]{1,0:T(8,128)(2,1)} %vec.3) | copy-start | bytes 49156
  15.8 2.2 %collective-permute-start = (bf16[8,8,1024]{2,1,0:T(8,128)(2,1)S(1)}, bf16[8,8,1024]{2,1,0:T(8,128)(2,1)S(1)}, u32[]{:S(2)}, u32[]{:S(2)}) collective-permute-start(bf16[8,8,1024]{2,1,0:T(8,128)(2,1)S(1)} %all_to_all.10.refs_0_), channel_id=1, source_target_pairs={{0,2},{2,0},{1,3},{3,1},{4,6},{6,4},{5,7},{7,5},{8,10},{10,8},{9,1... | collective-permute-start | bytes 393224 | tf_op jit(solution)/shard_map/ppermute | solution.py:302
  15.8 5.2 %collective-permute-start.1 = (bf16[8,1024]{1,0:T(8,128)(2,1)}, bf16[8,1024]{1,0:T(8,128)(2,1)S(1)}, u32[]{:S(2)}, u32[]{:S(2)}) collective-permute-start(bf16[8,1024]{1,0:T(8,128)(2,1)} %vec.3), channel_id=1, source_target_pairs={{0,1},{1,0},{2,3},{3,2},{4,5},{5,4},{6,7},{7,6},{8,9},{9,8},{10,11... | collective-permute-start | bytes 49160 | tf_op jit(solution)/shard_map/ppermute | solution.py:302
  22.0 11.8 %all-to-all-start.1 = ((f32[32,1,128]{2,1,0:T(1,128)}), f32[32,1,128]{2,1,0:T(1,128)S(1)}, u32[]{:S(2)}, u32[]{:S(2)}) async-start(f32[32,1,128]{2,1,0:T(1,128)} %broadcast_in_dim.20), calls=%async_computation.1 | async-start | bytes 32768 | tf_op jit(solution)/shard_map/all_to_all | solution.py:323
  26.6 3.9 %collective-permute-start.2 = (bf16[8,1024]{1,0:T(8,128)(2,1)S(1)}, bf16[8,1024]{1,0:T(8,128)(2,1)S(1)}, u32[]{:S(2)}, u32[]{:S(2)}) collective-permute-start(bf16[8,1024]{1,0:T(8,128)(2,1)S(1)} %bitcast.4), channel_id=1, source_target_pairs={{0,1},{1,0},{2,3},{3,2},{4,5},{5,4},{6,7},{7,6},{8,9},{9,8},{10,11... | collective-permute-start | bytes 49160 | tf_op jit(solution)/shard_map/ppermute | solution.py:316
